TPU v7x, 32 devices: a whole 2x2x4 slice. The times are simulated.
32 devices in a mesh: depth: 8 (over y, x, core), outer: 4 (over z).
Axes of the slice: x: 2, y: 2, z: 4, core: 2. Of those that a mesh axis runs over, the one named last changes fastest.
Arguments:
- density: float32 [256, 16, 1024], P(('depth', 'outer')), may hold values from -16 to 16
- materials: int32 [256, 4, 256], P(('depth', 'outer')), may hold values from 0 to 15
- colors: float32 [3, 16], replicated, may hold values from 0.1 to 1
- opacity: float32 [16], replicated, may hold values from 2e-05 to 0.003
Outputs:
- picture: float32 [3, 16384], P(None, ('depth', 'outer'))
All inputs are finite; a program needn't handle non-finite values.
Results may differ from a plain program's by a relative error of at most 0.0003.
Values sent between devices are 32-bit elements; how exact they have to be, the bound alone decides.
A program may use at most 64 MiB of HBM per device.

v0:
```python
import functools

import jax
import jax.numpy as jnp
from jax import lax
from jax.experimental import pallas as pl
from jax.experimental.pallas import tpu as pltpu
from jax.sharding import PartitionSpec as P

LIGHT_DIR = (0.64, 0.48, 0.6)
MESH = pl.DeviceIdType.MESH
LANES = 128
HALO = 4
BLOCK = 4
CHANNELS = 4


def shifted(values, amount, axis, at_low, at_high):
    length = values.shape[axis]
    moved = pltpu.roll(values, (-amount) % length, axis)
    index = lax.broadcasted_iota(jnp.int32, values.shape, axis)
    if amount < 0 and at_low:
        moved = jnp.where(index < -amount, 0.0, moved)
    if amount > 0 and at_high:
        moved = jnp.where(index >= length - amount, 0.0, moved)
    return moved


def render_kernel(
    plan, density, materials, colors, opacity, out, ext, first, second, labels, spread, coarse, table,
    pieces, inbox, own_sem, label_sem, halo_send, halo_recv, piece_send, piece_recv,
):
    count, group, direct = plan["count"], plan["group"], plan["direct"]
    depth_own, rows, cols = density.shape
    depth_at, outer_at = lax.axis_index("depth"), lax.axis_index("outer")
    me = depth_at * group + outer_at
    planes = depth_own + 2 * HALO

    def device(position):
        return (lax.div(position, group), lax.rem(position, group))

    own_copy = pltpu.make_async_copy(density, ext.at[pl.ds(HALO, depth_own)], own_sem)
    own_copy.start()
    label_copy = pltpu.make_async_copy(materials, labels, label_sem)
    label_copy.start()

    barrier = pltpu.get_barrier_semaphore()
    if direct:
        @pl.loop(1, count)
        def _(step):
            pl.semaphore_signal(barrier, inc=1, device_id=device(lax.rem(me + step, count)), device_id_type=MESH)
        pl.semaphore_wait(barrier, count - 1)
    else:
        for away, there in ((-1, me > 0), (1, me < count - 1)):
            @pl.when(there)
            def _(away=away):
                pl.semaphore_signal(barrier, inc=1, device_id=device(me + away), device_id_type=MESH)
        for there in (me > 0, me < count - 1):
            @pl.when(there)
            def _():
                pl.semaphore_wait(barrier, 1)

    width = plan["width"]
    chunks = cols // width
    ends = [min((at + 1) * width + LANES, cols) for at in range(chunks)]
    begins = [0] + ends[:-1]

    def halo_copy(side, at):
        lanes = pl.ds(begins[at], ends[at] - begins[at])
        if side == 0:
            source, target, to = depth_own - HALO, 0, lax.rem(me + 1, count)
        else:
            source, target, to = 0, depth_own + HALO, lax.rem(me + count - 1, count)
        return pltpu.make_async_remote_copy(
            src_ref=density.at[pl.ds(source, HALO), :, lanes],
            dst_ref=ext.at[pl.ds(target, HALO), :, lanes],
            send_sem=halo_send.at[side, at],
            recv_sem=halo_recv.at[side, at],
            device_id=device(to),
            device_id_type=MESH,
        )

    sends = ((0, me < count - 1), (1, me > 0))
    receives = ((0, me > 0), (1, me < count - 1))
    for at in range(chunks):
        if begins[at] < ends[at]:
            for side, there in sends:
                @pl.when(there)
                def _(side=side, at=at):
                    halo_copy(side, at).start()

    @pl.when(me == 0)
    def _():
        ext[pl.ds(0, HALO)] = jnp.zeros((HALO, rows, cols), jnp.float32)

    @pl.when(me == count - 1)
    def _():
        ext[pl.ds(depth_own + HALO, HALO)] = jnp.zeros((HALO, rows, cols), jnp.float32)

    fine = BLOCK * LANES
    row_at = lax.rem(lax.broadcasted_iota(jnp.int32, (2 * LANES, fine), 0), LANES)
    col_at = lax.div(lax.broadcasted_iota(jnp.int32, (2 * LANES, fine), 1), BLOCK)
    spread[...] = jnp.where(row_at == col_at, 1.0, 0.0).astype(jnp.bfloat16)
    label_copy.wait()
    tiles = cols // fine

    @pl.loop(0, depth_own, unroll=2)
    def _(plane):
        index = labels[plane]
        index = jnp.concatenate(
            [jnp.broadcast_to(index[row : row + 1], (BLOCK, index.shape[1])) for row in range(rows // BLOCK)], 0
        )
        found = [jnp.zeros(index.shape, jnp.float32) for channel in range(CHANNELS)]
        for material in range(colors.shape[1]):
            chosen = index == material
            for channel in range(CHANNELS - 1):
                found[channel] = jnp.where(chosen, colors[channel, material], found[channel])
            found[-1] = jnp.where(chosen, 0.5 * opacity[material], found[-1])
        for channel in range(CHANNELS):
            high = found[channel].astype(jnp.bfloat16)
            low = (found[channel] - high.astype(jnp.float32)).astype(jnp.bfloat16)
            start = pl.multiple_of((plane * CHANNELS + channel) * rows, rows)
            for tile in range(tiles):
                lanes = slice(tile * LANES, (tile + 1) * LANES)
                coarse[tile, pl.ds(start, rows), :LANES] = high[:, lanes]
                coarse[tile, pl.ds(start, rows), LANES:] = low[:, lanes]

    for tile in range(tiles):
        table[:, tile * fine : (tile + 1) * fine] = jnp.dot(
            coarse[tile], spread[...], preferred_element_type=jnp.float32
        )

    def smooth(source, target, start, stop, low, high):
        lanes = pl.ds(low, high - low)

        @pl.loop(start, stop, unroll=True)
        def _(plane):
            where = me * depth_own - HALO + plane
            inside = jnp.where((where >= 0) & (where < count * depth_own), 1.0, 0.0)
            center = source[plane, :, lanes]
            beside = source[plane - 1, :, lanes] + source[plane + 1, :, lanes]
            beside += shifted(center, -1, 0, True, True) + shifted(center, 1, 0, True, True)
            beside += shifted(center, -1, 1, low == 0, high == cols) + shifted(center, 1, 1, low == 0, high == cols)
            target[plane, :, lanes] = (0.25 * inside) * center + (0.125 * inside) * beside

    own_copy.wait()
    smooth(ext, first, HALO + 1, planes - HALO - 1, 0, cols)
    smooth(first, second, HALO + 2, planes - HALO - 2, 0, cols)

    def differences(minus, plus, minus_two, plus_two):
        return ((plus - minus) + 2.0 * (plus_two - minus_two)) * 0.1

    block = min(width, 2 * LANES)
    for at in range(chunks):
        if begins[at] < ends[at]:
            for side, there in receives:
                @pl.when(there)
                def _(side=side, at=at):
                    halo_copy(side, at).wait_recv()
        low, high = max(at * width - LANES, 0), ends[at]
        smooth(ext, first, 1, HALO + 1, low, high)
        smooth(ext, first, planes - HALO - 1, planes - 1, low, high)
        smooth(first, second, 2, HALO + 2, low, high)
        smooth(first, second, planes - HALO - 2, planes - 2, low, high)
        for base in range(at * width, (at + 1) * width, block):
            left, right = max(base - LANES, 0), min(base + block + LANES, cols)

            def shade(plane, carry, base=base, left=left, right=right):
                light, transmit = carry[:3], carry[3]
                own = pl.ds(base, block)
                slot = plane + HALO
                center = second[slot, :, own]
                along = functools.partial(shifted, center, axis=0, at_low=True, at_high=True)
                wide = second[slot, :, pl.ds(left, right - left)]

                def across(amount):
                    moved = shifted(wide, amount, 1, left == 0, right == cols)
                    return moved[:, base - left : base - left + block]

                grad_depth = differences(*(second[slot + step, :, own] for step in (-1, 1, -2, 2)))
                grad_rows = differences(*(along(step) for step in (-1, 1, -2, 2)))
                grad_cols = differences(*(across(step) for step in (-1, 1, -2, 2)))
                facing = LIGHT_DIR[0] * grad_depth + LIGHT_DIR[1] * grad_rows + LIGHT_DIR[2] * grad_cols
                length_sq = grad_depth * grad_depth + grad_rows * grad_rows + grad_cols * grad_cols + 1.0
                shading = 0.1 + 0.9 * jnp.abs(facing) * lax.rsqrt(length_sq)

                def looked_up(channel):
                    start = pl.multiple_of((plane * CHANNELS + channel) * rows, rows)
                    return table[pl.ds(start, rows), own]

                stopped = transmit * (looked_up(3) * (1.0 + jnp.tanh(center)))
                shaded = stopped * shading
                light = tuple(light[channel] + looked_up(channel) * shaded for channel in range(3))
                return light + (transmit - stopped,)

            empty = jnp.zeros((rows, block), jnp.float32)
            layers = lax.fori_loop(0, depth_own, shade, (empty, empty, empty, empty + 1.0), unroll=True)
            for channel in range(CHANNELS):
                if not direct:
                    out[channel, :, pl.ds(base, block)] = layers[channel]
                    continue
                strips = width // LANES
                for strip in range(block // LANES):
                    slot = (base - at * width) // LANES + strip
                    start = at * CHANNELS * strips + channel * strips + slot
                    pieces[pl.ds(start, rows, stride=chunks * CHANNELS * strips), :] = layers[channel][
                        :, strip * LANES : (strip + 1) * LANES
                    ]
        if direct:
            size = CHANNELS * width // LANES

            @pl.loop(0, rows)
            def _(row, at=at):
                to = row * chunks + at
                here = pl.ds(pl.multiple_of(to * size, size), size)
                there = pl.ds(pl.multiple_of(me * size, size), size)

                @pl.when(to != me)
                def _():
                    pltpu.make_async_remote_copy(
                        src_ref=pieces.at[here],
                        dst_ref=inbox.at[there],
                        send_sem=piece_send,
                        recv_sem=piece_recv,
                        device_id=device(to),
                        device_id_type=MESH,
                    ).start()

                @pl.when(to == me)
                def _():
                    inbox[there, :] = pieces[here, :]

    if direct:
        size = CHANNELS * width // LANES
        strips = width // LANES
        others = pl.ds(0, (count - 1) * size)
        everything = pltpu.make_async_remote_copy(
            src_ref=pieces.at[others],
            dst_ref=inbox.at[others],
            send_sem=piece_send,
            recv_sem=piece_recv,
            device_id=device(lax.rem(me + 1, count)),
            device_id_type=MESH,
        )
        everything.wait_recv()
        total = [jnp.zeros((strips, LANES), jnp.float32) for channel in range(3)]
        left_over = jnp.ones((strips, LANES), jnp.float32)
        for source in range(count):
            base = source * size
            for channel in range(3):
                total[channel] += left_over * inbox[base + channel * strips : base + (channel + 1) * strips, :]
            left_over = left_over * inbox[base + 3 * strips : base + 4 * strips, :]
        for channel in range(3):
            toned = 1.0 - jnp.exp(-4.0 * total[channel])
            for strip in range(strips):
                out[channel : channel + 1, strip * LANES : (strip + 1) * LANES] = toned[strip : strip + 1]
        everything.wait_send()
    for at in range(chunks):
        if begins[at] < ends[at]:
            for side, there in sends:
                @pl.when(there)
                def _(side=side, at=at):
                    halo_copy(side, at).wait_send()


def over_blend(front_part, back_part):
    transmit = front_part[3:4]
    return jnp.concatenate([front_part[:3] + transmit * back_part[:3], transmit * back_part[3:4]], 0)


def blend_group(received):
    blended = received
    while blended.shape[2] > 1:
        channels, items, sources, owned = blended.shape
        paired = blended.reshape(channels, items, sources // 2, 2, owned)
        blended = over_blend(paired[:, :, :, 0, :], paired[:, :, :, 1, :])
    return blended[:, :, 0, :]


def on_device(density, materials, colors, opacity):
    depth_count, group = lax.axis_size("depth"), lax.axis_size("outer")
    count = depth_count * group
    depth_own, rows, cols = density.shape
    owned = rows * cols // count
    direct = owned % (2 * LANES) == 0 and cols % owned == 0
    width = owned if direct else cols
    size = CHANNELS * width // LANES if direct else 8
    planes = depth_own + 2 * HALO
    out_shape = (3, owned) if direct else (CHANNELS, rows, cols)
    chunks = cols // width
    volume = pltpu.VMEM((planes, rows, cols), jnp.float32)
    tiles = cols // (BLOCK * LANES)
    layers = pl.pallas_call(
        functools.partial(render_kernel, dict(count=count, group=group, direct=direct, width=width)),
        out_shape=jax.ShapeDtypeStruct(out_shape, jnp.float32),
        in_specs=[
            pl.BlockSpec(memory_space=pl.ANY),
            pl.BlockSpec(memory_space=pl.ANY),
            pl.BlockSpec(memory_space=pltpu.SMEM),
            pl.BlockSpec(memory_space=pltpu.SMEM),
        ],
        out_specs=pl.BlockSpec(memory_space=pltpu.VMEM),
        scratch_shapes=[
            volume,
            volume,
            volume,
            pltpu.VMEM(materials.shape, jnp.int32),
            pltpu.VMEM((2 * LANES, BLOCK * LANES), jnp.bfloat16),
            pltpu.VMEM((tiles, CHANNELS * depth_own * rows, 2 * LANES), jnp.bfloat16),
            pltpu.VMEM((CHANNELS * depth_own * rows, cols), jnp.float32),
            pltpu.VMEM((count * size, LANES), jnp.float32),
            pltpu.VMEM((count * size, LANES), jnp.float32),
            pltpu.SemaphoreType.DMA,
            pltpu.SemaphoreType.DMA,
            pltpu.SemaphoreType.DMA((2, chunks)),
            pltpu.SemaphoreType.DMA((2, chunks)),
            pltpu.SemaphoreType.DMA,
            pltpu.SemaphoreType.DMA,
        ],
        compiler_params=pltpu.CompilerParams(
            collective_id=0, has_side_effects=True, vmem_limit_bytes=60 * 1024 * 1024
        ),
    )(density, materials, colors, opacity)
    if direct:
        return layers
    layers = layers.reshape(CHANNELS, depth_count, group, owned)
    merged = blend_group(lax.all_to_all(layers, "outer", split_axis=2, concat_axis=2, tiled=True))
    stacked = merged.reshape(CHANNELS, 1, depth_count, owned)
    layers = blend_group(lax.all_to_all(stacked, "depth", split_axis=2, concat_axis=2, tiled=True))
    return 1.0 - jnp.exp(-4.0 * layers.reshape(CHANNELS, owned)[:3])


def solution(mesh):
    placed = (P(("depth", "outer"), None, None), P(("depth", "outer"), None, None), P(), P())
    return jax.shard_map(
        on_device,
        mesh=mesh,
        in_specs=placed,
        out_specs=P(None, ("depth", "outer")),
        check_vma=False,
    )
```

profile of v0, /device:TPU:0, one launch (start us, length us, event | category | flops | bytes accessed | tf_op | source)
XLA Modules:
  0.0 28.5 jit_solution(12372266872809573955)
XLA Ops:
  0.0 27.2 %shard_map.46 = f32[3,512]{1,0:T(4,128)} custom-call(f32[8,16,1024]{2,1,0:T(8,128)} %density.1, s32[8,4,256]{2,1,0:T(4,128)} %materials.1, f32[3,16]{1,0:T(4,128)} %colors.1, f32[16]{0:T(128)} %opacity.1), custom_call_target="tpu_custom_call" | custom-call | tf_op jit(solution)/shard_map/pallas_call | solution.py:293
  27.3 1.3 %copy.6 = f32[3,512]{1,0:T(4,128)} copy(f32[3,512]{1,0:T(4,128)} %shard_map.46) | data formatting | bytes 12288
where the time goes:
time: 28.8 us; the launch traced here: 28.5 us
  Pallas kernels  27.2 us (94%)
  local copies, waits for them, and re-layouts  1.3 us (5%)
    pallas_call x1, Pallas kernels, on_device(): pl.pallas_call(functools.partial(render_kernel, dict(count=count, group=g...  27.2 us
    unnamed x1, local copies, waits for them, and re-layouts  1.3 us

commit v1 on v0

--- a/solution.py
+++ b/solution.py
@@ -27,8 +27,8 @@
 
 
 def render_kernel(
-    plan, density, materials, colors, opacity, out, ext, first, second, labels, spread, coarse, table,
-    pieces, inbox, own_sem, label_sem, halo_send, halo_recv, piece_send, piece_recv,
+    plan, density, materials, colors_in, opacity_in, out, colors, opacity, ext, first, second, labels, spread, coarse, table,
+    pieces, inbox, own_sem, label_sem, color_sem, opacity_sem, halo_send, halo_recv, piece_send, piece_recv,
 ):
     count, group, direct = plan["count"], plan["group"], plan["direct"]
     depth_own, rows, cols = density.shape
@@ -43,6 +43,10 @@
     own_copy.start()
     label_copy = pltpu.make_async_copy(materials, labels, label_sem)
     label_copy.start()
+    color_copy = pltpu.make_async_copy(colors_in, colors, color_sem)
+    color_copy.start()
+    opacity_copy = pltpu.make_async_copy(opacity_in, opacity, opacity_sem)
+    opacity_copy.start()
 
     barrier = pltpu.get_barrier_semaphore()
     if direct:
@@ -82,12 +86,21 @@
 
     sends = ((0, me < count - 1), (1, me > 0))
     receives = ((0, me > 0), (1, me < count - 1))
-    for at in range(chunks):
-        if begins[at] < ends[at]:
-            for side, there in sends:
-                @pl.when(there)
-                def _(side=side, at=at):
-                    halo_copy(side, at).start()
+
+    def start_halo(at):
+        for side, there in sends:
+            @pl.when(there)
+            def _(side=side):
+                halo_copy(side, at).start()
+
+    def finish_halo(at):
+        for side, there in sends:
+            @pl.when(there)
+            def _(side=side):
+                halo_copy(side, at).wait_send()
+
+    used = [at for at in range(chunks) if begins[at] < ends[at]]
+    start_halo(used[0])
 
     @pl.when(me == 0)
     def _():
@@ -102,6 +115,8 @@
     col_at = lax.div(lax.broadcasted_iota(jnp.int32, (2 * LANES, fine), 1), BLOCK)
     spread[...] = jnp.where(row_at == col_at, 1.0, 0.0).astype(jnp.bfloat16)
     label_copy.wait()
+    color_copy.wait()
+    opacity_copy.wait()
     tiles = cols // fine
 
     @pl.loop(0, depth_own, unroll=2)
@@ -152,7 +167,10 @@
 
     block = min(width, 2 * LANES)
     for at in range(chunks):
-        if begins[at] < ends[at]:
+        if at in used:
+            if at != used[-1]:
+                finish_halo(at)
+                start_halo(used[used.index(at) + 1])
             for side, there in receives:
                 @pl.when(there)
                 def _(side=side, at=at):
@@ -211,7 +229,7 @@
 
             @pl.loop(0, rows)
             def _(row, at=at):
-                to = row * chunks + at
+                to = lax.rem(lax.div(me, chunks) + row, rows) * chunks + at
                 here = pl.ds(pl.multiple_of(to * size, size), size)
                 there = pl.ds(pl.multiple_of(me * size, size), size)
 
@@ -255,12 +273,7 @@
             for strip in range(strips):
                 out[channel : channel + 1, strip * LANES : (strip + 1) * LANES] = toned[strip : strip + 1]
         everything.wait_send()
-    for at in range(chunks):
-        if begins[at] < ends[at]:
-            for side, there in sends:
-                @pl.when(there)
-                def _(side=side, at=at):
-                    halo_copy(side, at).wait_send()
+    finish_halo(used[-1])
 
 
 def over_blend(front_part, back_part):
@@ -296,11 +309,13 @@
         in_specs=[
             pl.BlockSpec(memory_space=pl.ANY),
             pl.BlockSpec(memory_space=pl.ANY),
-            pl.BlockSpec(memory_space=pltpu.SMEM),
-            pl.BlockSpec(memory_space=pltpu.SMEM),
+            pl.BlockSpec(memory_space=pl.ANY),
+            pl.BlockSpec(memory_space=pl.ANY),
         ],
         out_specs=pl.BlockSpec(memory_space=pltpu.VMEM),
         scratch_shapes=[
+            pltpu.SMEM(colors.shape, jnp.float32),
+            pltpu.SMEM(opacity.shape, jnp.float32),
             volume,
             volume,
             volume,
@@ -310,6 +325,8 @@
             pltpu.VMEM((CHANNELS * depth_own * rows, cols), jnp.float32),
             pltpu.VMEM((count * size, LANES), jnp.float32),
             pltpu.VMEM((count * size, LANES), jnp.float32),
+            pltpu.SemaphoreType.DMA,
+            pltpu.SemaphoreType.DMA,
             pltpu.SemaphoreType.DMA,
             pltpu.SemaphoreType.DMA,
             pltpu.SemaphoreType.DMA((2, chunks)),

time: 28.8 us -> 28 us (0.972)
  the two profiles are of different devices: /device:TPU:0 before, /device:TPU:9 now
where the time goes in v1:
time: 28 us; the launch traced here: 27.8 us
  Pallas kernels  26.5 us (95%)
  local copies, waits for them, and re-layouts  1.3 us (5%)
    pallas_call x1, Pallas kernels, on_device(): pl.pallas_call(functools.partial(render_kernel, dict(count=count, group=g...  26.5 us
    unnamed x1, local copies, waits for them, and re-layouts  1.3 us

profile of v1, /device:TPU:9, one launch (start us, length us, event | category | flops | bytes accessed | tf_op | source)
XLA Modules:
  0.0 27.8 jit_solution(11350783903110748647)
XLA Ops:
  0.0 26.5 %shard_map.46 = f32[3,512]{1,0:T(4,128)} custom-call(f32[8,16,1024]{2,1,0:T(8,128)} %density.1, s32[8,4,256]{2,1,0:T(4,128)} %materials.1, f32[3,16]{1,0:T(4,128)} %colors_in.1, f32[16]{0:T(128)} %opacity_in.1), custom_call_target="tpu_custom_call" | custom-call | tf_op jit(solution)/shard_map/pallas_call | solution.py:306
  26.5 1.3 %copy.6 = f32[3,512]{1,0:T(4,128)} copy(f32[3,512]{1,0:T(4,128)} %shard_map.46) | data formatting | bytes 12288

commit v2 on v1

--- a/solution.py
+++ b/solution.py
@@ -64,7 +64,7 @@
             def _():
                 pl.semaphore_wait(barrier, 1)
 
-    width = plan["width"]
+    width, parts = plan["width"], plan["parts"]
     chunks = cols // width
     ends = [min((at + 1) * width + LANES, cols) for at in range(chunks)]
     begins = [0] + ends[:-1]
@@ -100,7 +100,8 @@
                 halo_copy(side, at).wait_send()
 
     used = [at for at in range(chunks) if begins[at] < ends[at]]
-    start_halo(used[0])
+    for at in used[:2]:
+        start_halo(at)
 
     @pl.when(me == 0)
     def _():
@@ -145,7 +146,7 @@
             coarse[tile], spread[...], preferred_element_type=jnp.float32
         )
 
-    def smooth(source, target, start, stop, low, high):
+    def smooth(source, target, start, stop, low, high, keep=0):
         lanes = pl.ds(low, high - low)
 
         @pl.loop(start, stop, unroll=True)
@@ -156,7 +157,8 @@
             beside = source[plane - 1, :, lanes] + source[plane + 1, :, lanes]
             beside += shifted(center, -1, 0, True, True) + shifted(center, 1, 0, True, True)
             beside += shifted(center, -1, 1, low == 0, high == cols) + shifted(center, 1, 1, low == 0, high == cols)
-            target[plane, :, lanes] = (0.25 * inside) * center + (0.125 * inside) * beside
+            smoothed = (0.25 * inside) * center + (0.125 * inside) * beside
+            target[plane, :, pl.ds(low + keep, high - low - keep)] = smoothed[:, keep:]
 
     own_copy.wait()
     smooth(ext, first, HALO + 1, planes - HALO - 1, 0, cols)
@@ -168,18 +170,19 @@
     block = min(width, 2 * LANES)
     for at in range(chunks):
         if at in used:
-            if at != used[-1]:
+            if used.index(at) + 2 < len(used):
                 finish_halo(at)
-                start_halo(used[used.index(at) + 1])
+                start_halo(used[used.index(at) + 2])
             for side, there in receives:
                 @pl.when(there)
                 def _(side=side, at=at):
                     halo_copy(side, at).wait_recv()
         low, high = max(at * width - LANES, 0), ends[at]
-        smooth(ext, first, 1, HALO + 1, low, high)
-        smooth(ext, first, planes - HALO - 1, planes - 1, low, high)
-        smooth(first, second, 2, HALO + 2, low, high)
-        smooth(first, second, planes - HALO - 2, planes - 2, low, high)
+        keep = at * width - low
+        smooth(ext, first, 1, HALO + 1, low, high, keep)
+        smooth(ext, first, planes - HALO - 1, planes - 1, low, high, keep)
+        smooth(first, second, 2, HALO + 2, low, high, keep)
+        smooth(first, second, planes - HALO - 2, planes - 2, low, high, keep)
         for base in range(at * width, (at + 1) * width, block):
             left, right = max(base - LANES, 0), min(base + block + LANES, cols)
 
@@ -229,9 +232,10 @@
 
             @pl.loop(0, rows)
             def _(row, at=at):
-                to = lax.rem(lax.div(me, chunks) + row, rows) * chunks + at
-                here = pl.ds(pl.multiple_of(to * size, size), size)
-                there = pl.ds(pl.multiple_of(me * size, size), size)
+                to_row = lax.rem(lax.div(me, chunks // parts) + row, rows)
+                to = to_row * (chunks // parts) + at // parts
+                here = pl.ds(pl.multiple_of((to_row * chunks + at) * size, size), size)
+                there = pl.ds(pl.multiple_of((me * parts + at % parts) * size, size), size)
 
                 @pl.when(to != me)
                 def _():
@@ -251,7 +255,7 @@
     if direct:
         size = CHANNELS * width // LANES
         strips = width // LANES
-        others = pl.ds(0, (count - 1) * size)
+        others = pl.ds(0, (count - 1) * parts * size)
         everything = pltpu.make_async_remote_copy(
             src_ref=pieces.at[others],
             dst_ref=inbox.at[others],
@@ -261,19 +265,22 @@
             device_id_type=MESH,
         )
         everything.wait_recv()
-        total = [jnp.zeros((strips, LANES), jnp.float32) for channel in range(3)]
-        left_over = jnp.ones((strips, LANES), jnp.float32)
-        for source in range(count):
-            base = source * size
+        for part in range(parts):
+            total = [jnp.zeros((strips, LANES), jnp.float32) for channel in range(3)]
+            left_over = jnp.ones((strips, LANES), jnp.float32)
+            for source in range(count):
+                base = (source * parts + part) * size
+                for channel in range(3):
+                    total[channel] += left_over * inbox[base + channel * strips : base + (channel + 1) * strips, :]
+                left_over = left_over * inbox[base + 3 * strips : base + 4 * strips, :]
             for channel in range(3):
-                total[channel] += left_over * inbox[base + channel * strips : base + (channel + 1) * strips, :]
-            left_over = left_over * inbox[base + 3 * strips : base + 4 * strips, :]
-        for channel in range(3):
-            toned = 1.0 - jnp.exp(-4.0 * total[channel])
-            for strip in range(strips):
-                out[channel : channel + 1, strip * LANES : (strip + 1) * LANES] = toned[strip : strip + 1]
+                toned = 1.0 - jnp.exp(-4.0 * total[channel])
+                for strip in range(strips):
+                    lane = part * width + strip * LANES
+                    out[channel : channel + 1, lane : lane + LANES] = toned[strip : strip + 1]
         everything.wait_send()
-    finish_halo(used[-1])
+    for at in used[-2:]:
+        finish_halo(at)
 
 
 def over_blend(front_part, back_part):
@@ -296,7 +303,8 @@
     depth_own, rows, cols = density.shape
     owned = rows * cols // count
     direct = owned % (2 * LANES) == 0 and cols % owned == 0
-    width = owned if direct else cols
+    width = 2 * LANES if direct else cols
+    parts = owned // width if direct else 1
     size = CHANNELS * width // LANES if direct else 8
     planes = depth_own + 2 * HALO
     out_shape = (3, owned) if direct else (CHANNELS, rows, cols)
@@ -304,7 +312,7 @@
     volume = pltpu.VMEM((planes, rows, cols), jnp.float32)
     tiles = cols // (BLOCK * LANES)
     layers = pl.pallas_call(
-        functools.partial(render_kernel, dict(count=count, group=group, direct=direct, width=width)),
+        functools.partial(render_kernel, dict(count=count, group=group, direct=direct, width=width, parts=parts)),
         out_shape=jax.ShapeDtypeStruct(out_shape, jnp.float32),
         in_specs=[
             pl.BlockSpec(memory_space=pl.ANY),
@@ -323,8 +331,8 @@
             pltpu.VMEM((2 * LANES, BLOCK * LANES), jnp.bfloat16),
             pltpu.VMEM((tiles, CHANNELS * depth_own * rows, 2 * LANES), jnp.bfloat16),
             pltpu.VMEM((CHANNELS * depth_own * rows, cols), jnp.float32),
-            pltpu.VMEM((count * size, LANES), jnp.float32),
-            pltpu.VMEM((count * size, LANES), jnp.float32),
+            pltpu.VMEM((count * parts * size, LANES), jnp.float32),
+            pltpu.VMEM((count * parts * size, LANES), jnp.float32),
             pltpu.SemaphoreType.DMA,
             pltpu.SemaphoreType.DMA,
             pltpu.SemaphoreType.DMA,

time: 28 us -> 28.4 us (1.014)
  the two profiles are of different devices: /device:TPU:9 before, /device:TPU:0 now
where the time goes in v2:
time: 28.4 us; the launch traced here: 28.2 us
  Pallas kernels  26.9 us (95%)
  local copies, waits for them, and re-layouts  1.3 us (5%)
    pallas_call x1, Pallas kernels, on_device(): pl.pallas_call(functools.partial(render_kernel, dict(count=count, group=g...  26.9 us
    unnamed x1, local copies, waits for them, and re-layouts  1.3 us

profile of v2, /device:TPU:0, one launch (start us, length us, event | category | flops | bytes accessed | tf_op | source)
XLA Modules:
  0.0 28.2 jit_solution(12818520106307002172)
XLA Ops:
  0.0 26.9 %shard_map.46 = f32[3,512]{1,0:T(4,128)} custom-call(f32[8,16,1024]{2,1,0:T(8,128)} %density.1, s32[8,4,256]{2,1,0:T(4,128)} %materials.1, f32[3,16]{1,0:T(4,128)} %colors_in.1, f32[16]{0:T(128)} %opacity_in.1), custom_call_target="tpu_custom_call" | custom-call | tf_op jit(solution)/shard_map/pallas_call | solution.py:314
  26.9 1.3 %copy.6 = f32[3,512]{1,0:T(4,128)} copy(f32[3,512]{1,0:T(4,128)} %shard_map.46) | data formatting | bytes 12288

commit v3 on v1

--- a/solution.py
+++ b/solution.py
@@ -50,7 +50,7 @@
 
     barrier = pltpu.get_barrier_semaphore()
     if direct:
-        @pl.loop(1, count)
+        @pl.loop(1, count, unroll=True)
         def _(step):
             pl.semaphore_signal(barrier, inc=1, device_id=device(lax.rem(me + step, count)), device_id_type=MESH)
         pl.semaphore_wait(barrier, count - 1)
@@ -100,7 +100,8 @@
                 halo_copy(side, at).wait_send()
 
     used = [at for at in range(chunks) if begins[at] < ends[at]]
-    start_halo(used[0])
+    for at in used:
+        start_halo(at)
 
     @pl.when(me == 0)
     def _():
@@ -168,9 +169,6 @@
     block = min(width, 2 * LANES)
     for at in range(chunks):
         if at in used:
-            if at != used[-1]:
-                finish_halo(at)
-                start_halo(used[used.index(at) + 1])
             for side, there in receives:
                 @pl.when(there)
                 def _(side=side, at=at):
@@ -273,7 +271,8 @@
             for strip in range(strips):
                 out[channel : channel + 1, strip * LANES : (strip + 1) * LANES] = toned[strip : strip + 1]
         everything.wait_send()
-    finish_halo(used[-1])
+    for at in used:
+        finish_halo(at)
 
 
 def over_blend(front_part, back_part):

time: 28 us -> 27.8 us (level)
  the two profiles are of different devices: /device:TPU:9 before, /device:TPU:0 now
where the time goes in v3:
time: 27.8 us; the launch traced here: 27.6 us
  Pallas kernels  26.3 us (95%)
  local copies, waits for them, and re-layouts  1.3 us (5%)
    pallas_call x1, Pallas kernels, on_device(): pl.pallas_call(functools.partial(render_kernel, dict(count=count, group=g...  26.3 us
    unnamed x1, local copies, waits for them, and re-layouts  1.3 us

profile of v3, /device:TPU:0, one launch (start us, length us, event | category | flops | bytes accessed | tf_op | source)
XLA Modules:
  0.0 27.6 jit_solution(6888184759686753445)
XLA Ops:
  0.0 26.3 %shard_map.46 = f32[3,512]{1,0:T(4,128)} custom-call(f32[8,16,1024]{2,1,0:T(8,128)} %density.1, s32[8,4,256]{2,1,0:T(4,128)} %materials.1, f32[3,16]{1,0:T(4,128)} %colors_in.1, f32[16]{0:T(128)} %opacity_in.1), custom_call_target="tpu_custom_call" | custom-call | tf_op jit(solution)/shard_map/pallas_call | solution.py:305
  26.3 1.3 %copy.6 = f32[3,512]{1,0:T(4,128)} copy(f32[3,512]{1,0:T(4,128)} %shard_map.46) | data formatting | bytes 12288
